TPU v7x, 256 devices: a whole 4x4x8 slice. The times are simulated.
256 devices in a mesh: dp: 64 (over z, y, core), group: 4 (over x).
Axes of the slice: x: 4, y: 4, z: 8, core: 2. Of those that a mesh axis runs over, the one named last changes fastest.
Arguments:
- features: bfloat16 [256, 1536, 1024], P(('dp', 'group')), may hold values from -6 to 6
- targets: int32 [256, 4, 1536], P(('dp', 'group')), may hold values from 0 to 1024, as said below
- matches: int32 [256, 1536], P(('dp', 'group')), may hold values from -1 to 383, as said below
- queries: bfloat16 [24576, 768], P(('dp', 'group')), may hold values from -6 to 6
- class_weight: bfloat16 [1024, 768], replicated, may hold values from -0.1875 to 0.1875
- trunk_weight: bfloat16 [1024, 1024], replicated, may hold values from -0.1875 to 0.1875
- head_rows: bfloat16 [6, 1024], replicated
Outputs:
- loss: float32 [], replicated
- query_grad: float32 [24576, 768], P(('dp', 'group'))
- class_grad: float32 [1024, 768], P('dp')
- box_grad: float32 [4, 1024], replicated
- side_grad: float32 [2, 1024], replicated
Inputs may be any that keep to these rules, and one draw needn't show every extreme that they name: `matches`: -1 marks a box matched to no query; any other value is the matched query's index among the 384 queries of the image's group; every image has 32 or more matched boxes. `targets`: the four rows are left, top, right, bottom in units of 1 / 1024 of the image side; right - left and bottom - top are 64 or more.
All inputs are finite; a program needn't handle non-finite values.
Results may differ from a plain program's by a relative error of at most 0.013.
Values may be sent and summed in bfloat16 or wider, within the bound.
A program may use at most 64 MiB of HBM per device.

v0:
```python
import jax
import jax.numpy as jnp
from jax import lax
from jax.sharding import PartitionSpec as P

GRID = 72
QUANT = 1024


ALPHA = 0.25
GIOU_WEIGHT = 2.0
LOGIT_BIAS = -4.0
EPSILON = 1e-06


def contract(left, right, left_dim, right_dim):
    return lax.dot_general(
        left, right, (((left_dim,), (right_dim,)), ((), ())), preferred_element_type=jnp.float32
    )


def logit(value):
    return jnp.log(value) - jnp.log1p(-value)


def box_prior(length):
    index = jnp.arange(length, dtype=jnp.int32)
    column = (index % GRID).astype(jnp.float32)
    line = (index // GRID).astype(jnp.float32)
    across = logit((column + 0.5) / GRID)
    down = logit((line + 0.5) / GRID)
    size = logit(jnp.full((length,), 1.0 / GRID, jnp.float32))
    return jnp.stack([across, down, size, size], 0)


def box_loss(box_raw, corners, weight):
    box = jax.nn.sigmoid(box_raw)
    left = box[0] - 0.5 * box[2]
    right = box[0] + 0.5 * box[2]
    top = box[1] - 0.5 * box[3]
    bottom = box[1] + 0.5 * box[3]
    inter_w = jnp.maximum(jnp.minimum(right, corners[2]) - jnp.maximum(left, corners[0]), 0.0)
    inter_h = jnp.maximum(jnp.minimum(bottom, corners[3]) - jnp.maximum(top, corners[1]), 0.0)
    inter = inter_w * inter_h
    union = box[2] * box[3] + (corners[2] - corners[0]) * (corners[3] - corners[1]) - inter
    outer_w = jnp.maximum(right, corners[2]) - jnp.minimum(left, corners[0])
    outer_h = jnp.maximum(bottom, corners[3]) - jnp.minimum(top, corners[1])
    enclose = outer_w * outer_h
    giou = inter / union - (enclose - union) / enclose
    return jnp.sum(weight * (1.0 - giou))


def focal_parts(logits, is_match):
    prob = jax.nn.sigmoid(logits)
    log_pos = jax.nn.log_sigmoid(logits)
    log_neg = jax.nn.log_sigmoid(-logits)
    other = 1.0 - prob
    loss_pos = -ALPHA * other * other * log_pos
    loss_neg = -(1.0 - ALPHA) * prob * prob * log_neg
    grad_pos = ALPHA * other * other * (2.0 * prob * log_pos - other)
    grad_neg = (1.0 - ALPHA) * prob * prob * (prob - 2.0 * other * log_neg)
    total = jnp.sum(jnp.where(is_match, loss_pos, loss_neg))
    return (total, jnp.where(is_match, grad_pos, grad_neg))


def image_terms(
    features_one, corners_int, matches_one, group_queries, class_weight, trunk_weight, head_rows
):
    length = features_one.shape[0]
    width = group_queries.shape[0]
    hidden = jax.nn.gelu(
        jnp.dot(features_one, trunk_weight, preferred_element_type=jnp.float32)
    ).astype(jnp.bfloat16)
    embedding = jnp.dot(features_one, class_weight, preferred_element_type=jnp.float32)
    embed_norms = jnp.sqrt(jnp.sum(embedding * embedding, axis=1, keepdims=True) + EPSILON)
    exact_units = embedding / embed_norms
    units = exact_units.astype(jnp.bfloat16)
    box_raw = contract(head_rows[0:4], hidden, 1, 1) + box_prior(length)
    side = contract(head_rows[4:6], features_one, 1, 1)
    shift = side[0] + LOGIT_BIAS
    scale_pre = side[1]
    scale = jax.nn.elu(scale_pre) + 1.0
    cosine = contract(units, group_queries, 1, 1)
    logits = (cosine + shift[:, None]) * scale[:, None]
    is_match = matches_one[:, None] == jnp.arange(width, dtype=jnp.int32)[None, :]
    focal_sum, dlogits = focal_parts(logits, is_match)
    grad_logits = (dlogits * scale[:, None]).astype(jnp.bfloat16)
    d_shift = jnp.sum(dlogits, axis=1)
    d_scale = jnp.sum(dlogits * (cosine + shift[:, None]), axis=1)
    d_scale_pre = d_scale * jnp.where(scale_pre > 0, 1.0, jnp.exp(scale_pre))
    corners = corners_int.astype(jnp.float32) / QUANT
    weight = (matches_one >= 0).astype(jnp.float32)
    giou_sum, pullback = jax.vjp(lambda value: box_loss(value, corners, weight), box_raw)
    d_raw = GIOU_WEIGHT * pullback(jnp.ones_like(giou_sum))[0]
    row_grads = jnp.concatenate([d_raw, d_shift[None, :], d_scale_pre[None, :]], 0).astype(
        jnp.bfloat16
    )
    small_terms = jnp.concatenate(
        [contract(row_grads[0:4], hidden, 1, 0), contract(row_grads[4:6], features_one, 1, 0)], 0
    )
    d_units = jnp.dot(grad_logits, group_queries, preferred_element_type=jnp.float32)
    d_embedding = (
        (d_units - exact_units * jnp.sum(exact_units * d_units, axis=1, keepdims=True))
        / embed_norms
    ).astype(jnp.bfloat16)
    return (focal_sum, giou_sum, grad_logits, units, d_embedding, small_terms)


def on_device(features, targets, matches, queries, class_weight, trunk_weight, head_rows):
    features_one = features[0]
    matches_one = matches[0]
    count_local = jnp.sum((matches_one >= 0).astype(jnp.float32))
    positives = lax.psum(count_local, ("dp", "group"))
    exact_in = queries.astype(jnp.float32)
    query_norms = jnp.sqrt(jnp.sum(exact_in * exact_in, axis=1, keepdims=True) + EPSILON)
    exact_queries = exact_in / query_norms
    unit_queries = exact_queries.astype(jnp.bfloat16)
    group_queries = lax.all_gather(unit_queries, "group", axis=0, tiled=True)
    focal_local, giou_local, grad_logits, units, d_embedding, small_local = image_terms(
        features_one, targets[0], matches_one, group_queries, class_weight, trunk_weight, head_rows
    )
    query_sums = lax.psum_scatter(
        contract(grad_logits, units, 0, 0).astype(jnp.bfloat16),
        "group",
        scatter_dimension=0,
        tiled=True,
    ).astype(jnp.float32)
    share = class_weight.shape[0] // lax.axis_size("dp")
    summed = lax.psum(contract(features_one, d_embedding, 0, 0), ("dp", "group"))
    class_part = lax.dynamic_slice_in_dim(summed, lax.axis_index("dp") * share, share, 0)
    focal_all, giou_all, small_all = lax.psum(
        (focal_local, giou_local, small_local), ("dp", "group")
    )
    loss = (focal_all + GIOU_WEIGHT * giou_all) / positives
    query_grad = (
        (query_sums - exact_queries * jnp.sum(exact_queries * query_sums, axis=1, keepdims=True))
        / query_norms
        / positives
    )
    return (
        loss,
        query_grad,
        class_part / positives,
        small_all[0:4] / positives,
        small_all[4:6] / positives,
    )


def solution(mesh):
    in_specs = (
        P(("dp", "group"), None, None),
        P(("dp", "group"), None, None),
        P(("dp", "group"), None),
        P(("dp", "group"), None),
        P(),
        P(),
        P(),
    )
    out_specs = (P(), P(("dp", "group"), None), P("dp", None), P(), P())
    return jax.shard_map(
        on_device, mesh=mesh, in_specs=in_specs, out_specs=out_specs, check_vma=False
    )
```

profile of v0, /device:TPU:2, one launch (start us, length us, event | category | flops | bytes accessed | tf_op | source)
XLA Modules:
  0.0 333.5 jit_solution(2110934225483168531)
XLA Ops:
  8.0 0.0 copy-start
  8.0 0.0 copy-start.1
  8.0 0.0 reduce-scatter.2.cloned.1.call-start
  8.1 0.0 copy-start.5
  8.1 1.2 fusion.41
  9.3 0.7 copy-done
  10.0 1.6 fusion.14
  11.6 0.0 copy-done.1
  11.7 0.1 fusion.100
  11.8 14.5 %all_gather.3 = bf16[384,768]{1,0:T(8,128)(2,1)} all-gather(bf16[96,768]{1,0:T(8,128)(2,1)S(1)} %fusion.100), channel_id=1, replica_groups=mesh['dp'=64,'group'=4] {'group'}, dimensions={0}, use_global_device_ids=true | all-gather | bytes 737280 | tf_op jit(solution)/shard_map/all_gather | solution.py:118
  26.2 0.0 copy-done.5
  26.2 0.0 copy-start.3
  26.2 4.4 %multiply_reduce_fusion.1 = (f32[1536]{0:T(1024)S(1)}, f32[1536,768]{0,1:T(8,128)}) fusion(bf16[1024,768]{1,0:T(8,128)(2,1)S(1)} %copy-done.5, bf16[1,1536,1024]{2,1,0:T(8,128)(2,1)S(1)} %copy-done), kind=kOutput, calls=%fused_computation.13 | convolution fusion | flops 2418276864 | bytes 9443328 | tf_op jit(solution)/shard_map/dot_general | solution.py:74
  30.6 0.0 copy-done.3
  30.6 0.0 copy-start.6
  30.7 9.0 %fusion.101 = (bf16[1536]{0:T(1024)(128)(2,1)S(1)}, f32[1536]{0:T(1024)S(1)}, f32[]{:T(128)}, f32[1536,384]{0,1:T(8,128)S(1)}) fusion(f32[1536]{0:T(1024)S(1)} %get-tuple-element.68, s32[1536]{0:T(1024)S(1)} %reduce, f32[1536]{0:T(1024)S(1)} %get-tuple-element.18, bf16[384,768]{1,0:T(8,128)(2,1)} %all_gather.3, f32[1536,768]{0,1:T(8,128)} %get-tuple-element.65, ...), kind=kOutput, calls=%fused_computation.195 | convolution fusion | flops 934867968 | bytes 7701508 | tf_op jit(solution)/shard_map/dot_general | solution.py:17
  39.7 0.0 copy-start.7
  39.7 1.4 copy-done.7
  41.1 0.0 copy-done.6
  41.1 2.0 convolution_convert_fusion
  43.2 0.0 reduce-scatter.2.cloned.1.call-update
  43.2 0.2 all-reduce.13.cloned.1.call-start
  43.4 4.8 %multiply_reduce_fusion = (f32[1536]{0:T(1024)S(1)}, f32[1536,768]{0,1:T(8,128)S(1)}) fusion(f32[1536,768]{0,1:T(8,128)} %get-tuple-element.65, f32[1536]{0:T(1024)S(1)} %get-tuple-element.69, bf16[384,768]{1,0:T(8,128)(2,1)} %all_gather.3, f32[1536,384]{0,1:T(8,128)} %copy-done.7, f32[1536]{0:T(1024)S(1)} %get-tuple-element.68), kind=kOutput, calls=%fused_computation.12 | convolution fusion | flops 910686720 | bytes 12404736 | tf_op jit(solution)/shard_map/dot_general | solution.py:101
  48.2 6.6 %fusion.35 = f32[1024,768]{0,1:T(8,128)} fusion(bf16[1,1536,1024]{2,1,0:T(8,128)(2,1)S(1)} %copy-done, f32[1536,768]{0,1:T(8,128)S(1)} %get-tuple-element.67, f32[1536]{0:T(1024)S(1)} %get-tuple-element.66, f32[1536]{0:T(1024)S(1)} %get-tuple-element.69, f32[1536,768]{0,1:T(8,128)} %get-tuple-element.65), kind=kOutput, calls=%fused_computation.51 | convolution fusion | flops 2421817344 | bytes 15740928 | tf_op jit(solution)/shard_map/dot_general | solution.py:17
  54.8 0.0 copy-start.4
  54.8 0.0 all-reduce.13.cloned.1.call-update
  54.9 0.1 log-plus-one_subtract_fusion
  54.9 0.6 copy-done.4
  55.6 0.0 copy-start.2
  55.6 6.3 %fusion.7 = bf16[1536,1024]{1,0:T(8,128)(2,1)S(1)} fusion(bf16[1024,1024]{1,0:T(8,128)(2,1)} %param.12, bf16[1,1536,1024]{2,1,0:T(8,128)(2,1)S(1)} %copy-done), kind=kOutput, calls=%fused_computation.10 | convolution fusion | flops 3235381248 | bytes 8388608 | tf_op jit(solution)/shard_map/dot_general | solution.py:72
  62.0 0.0 copy-done.2
  62.0 0.9 fusion.34
  62.9 0.1 slice_multiply_fusion.1
  63.0 0.1 slice_multiply_fusion
  63.1 0.1 negate_multiply_fusion.1
  63.3 0.5 fusion.47
  63.8 0.5 fusion.8
  64.4 0.1 slice_reduce_fusion.4
  64.4 0.6 convert_reduce_fusion
  65.0 79.5 %all-reduce.10 = (f32[]{:T(128)}, f32[]{:T(128)}, f32[]{:T(128)}, f32[6,1024]{1,0:T(8,128)S(1)}) all-reduce(f32[]{:T(128)} %get-tuple-element.12, f32[]{:T(128)} %get-tuple-element.20, f32[]{:T(128)} %get-tuple-element.19, f32[6,1024]{1,0:T(8,128)S(1)} %pad_maximum_fusion), channel_id=1, replica_groups=mesh['dp'=64,'group'=4] {'dp','group'}, use_global_device_ids=true, to_apply=%region_3.0 | all-reduce | flops 6147 | bytes 49176 | tf_op jit(solution)/shard_map/psum | solution.py:131
  146.5 0.7 broadcast_multiply_fusion.2
  147.2 1.3 slice_divide_fusion.1
  148.4 1.3 slice_divide_fusion
  149.7 0.0 reduce-scatter.2.cloned.1.call-done
  149.7 1.1 fusion.42
  150.8 1.8 fusion.43
  152.6 169.7 %all-reduce.13.cloned.1.call-done = f32[1024,768]{0,1:T(8,128)} async-done(((f32[1024,768]{0,1:T(8,128)}), f32[1024,768]{0,1:T(8,128)}) %all-reduce.13.cloned.1.call-update) | async-done | bytes 3145744 | tf_op jit(solution)/shard_map/psum | solution.py:129
  322.3 1.8 dynamic-slice_divide_fusion
  324.2 0.8 copy.12
  (9 shorter events, 0.1 us)
Async XLA Ops:
  8.0 2.0 copy-start
  8.0 3.6 %copy-start.1 = (bf16[96,768]{1,0:T(8,128)(2,1)S(1)}, bf16[96,768]{1,0:T(8,128)(2,1)}, u32[]{:S(2)}) copy-start(bf16[96,768]{1,0:T(8,128)(2,1)} %param.10) | copy-start | bytes 442372
  8.0 141.7 %reduce-scatter.2.cloned.1.call-start = ((), (), s32[]{:S(2)}) async-start(), calls=%async_computation.1 | async-start | bytes 737280 | tf_op jit(solution)/shard_map/reduce_scatter | solution.py:122
  8.1 18.2 %copy-start.5 = (bf16[1024,768]{1,0:T(8,128)(2,1)S(1)}, bf16[1024,768]{1,0:T(8,128)(2,1)}, u32[]{:S(2)}) copy-start(bf16[1024,768]{1,0:T(8,128)(2,1)} %param.11) | copy-start | bytes 4718596
  26.2 4.4 %copy-start.3 = (s32[1,1536]{1,0:T(1,128)S(1)}, s32[1,1536]{1,0:T(1,128)}, u32[]{:S(2)}) copy-start(s32[1,1536]{1,0:T(1,128)} %param.9) | copy-start | bytes 18436
  30.6 10.5 %copy-start.6 = (f32[1536,768]{0,1:T(8,128)S(1)}, f32[1536,768]{0,1:T(8,128)}, u32[]{:S(2)}) copy-start(f32[1536,768]{0,1:T(8,128)} %get-tuple-element.65) | copy-start | bytes 14155780
  39.7 1.4 copy-start.7
  43.2 279.2 %all-reduce.13.cloned.1.call-start = ((), (), s32[]{:S(2)}) async-start(), calls=%async_computation.2 | async-start | bytes 6291456 | tf_op jit(solution)/shard_map/psum | solution.py:129
  54.8 0.7 copy-start.4
  55.6 6.4 %copy-start.2 = (bf16[6,1024]{1,0:T(8,128)(2,1)S(1)}, bf16[6,1024]{1,0:T(8,128)(2,1)}, u32[]{:S(2)}) copy-start(bf16[6,1024]{1,0:T(8,128)(2,1)} %param.13) | copy-start | bytes 36868
Sparse Core Ops, SparseCore 0:
  43.3 24.7 reduce-scatter.1
Sparse Core Ops, SparseCore 1:
  54.9 267.3 all-reduce.12
where the time goes:
time: 334 us; the launch traced here: 333 us
  waiting for transfers between devices  170 us (51%)
  blocking collectives  94 us (28%)
  matrix products  36.7 us (11%)
  between operations  18.8 us (6%)
  other arithmetic  10.4 us (3%)
  local copies, waits for them, and re-layouts  3.61 us (1%)
    psum x1, waiting for transfers between devices, on_device(): lax.psum(contract(features_one, d_embedding, 0, 0), ('dp', 'group'))  170 us
    psum x1, blocking collectives, on_device(): lax.psum((focal_local, giou_local, small_local), ('dp', 'group'))  79.5 us
    dot_general x7, matrix products, contract(): lax.dot_general(left, right, (((left_dim,), (right_dim,)), ((), ())), pre...  21.3 us
    all_gather x1, blocking collectives, on_device(): group_queries = lax.all_gather(unit_queries, 'group', axis=0, tiled=True)  14.5 us
  transfers between devices with their start and end apart: 2, of which 1 were waited for; matrix products, arithmetic and copies ran while one was open for 8% of the time, Pallas kernels for 0%

commit v1 on v0

v1 whole, which is shorter than its diff:
```python
import functools

import jax
import jax.numpy as jnp
import numpy as np
from jax import lax
from jax.experimental import pallas as pl
from jax.experimental.pallas import tpu as pltpu
from jax.sharding import PartitionSpec as P

MESH = pl.DeviceIdType.MESH
F32 = jnp.float32
BF16 = jnp.bfloat16

GRID = 72
QUANT = 1024
ALPHA = 0.25
GIOU_WEIGHT = 2.0
LOGIT_BIAS = -4.0
EPSILON = 1e-06

NX, NY, NZ, NC = 4, 4, 8, 2
E, D, ROWS, Q = 1024, 768, 1536, 384
QROWS = Q // NX
SHARE = E // (NZ * NY * NC)
HALF = D // 2
BLOCK = 256
PEERS = 1 + (NX - 1) + (NY - 1) + (NZ - 1)


def contract(left, right, left_dim, right_dim):
    return lax.dot_general(
        left, right, (((left_dim,), (right_dim,)), ((), ())), preferred_element_type=F32
    )


def box_prior(length):
    index = np.arange(length)

    def logit(value):
        return np.log(value) - np.log1p(-value)

    across = logit((index % GRID + 0.5) / GRID)
    down = logit((index // GRID + 0.5) / GRID)
    size = np.full((length,), logit(1.0 / GRID))
    return np.stack([across, down, size, size], 0).astype(np.float32)


def box_loss(box_raw, corners, weight):
    box = jax.nn.sigmoid(box_raw)
    cx, cy, bw, bh = (box[i : i + 1] for i in range(4))
    c0, c1, c2, c3 = (corners[i : i + 1] for i in range(4))
    left = cx - 0.5 * bw
    right = cx + 0.5 * bw
    top = cy - 0.5 * bh
    bottom = cy + 0.5 * bh
    inter_w = jnp.maximum(jnp.minimum(right, c2) - jnp.maximum(left, c0), 0.0)
    inter_h = jnp.maximum(jnp.minimum(bottom, c3) - jnp.maximum(top, c1), 0.0)
    inter = inter_w * inter_h
    union = bw * bh + (c2 - c0) * (c3 - c1) - inter
    outer_w = jnp.maximum(right, c2) - jnp.minimum(left, c0)
    outer_h = jnp.maximum(bottom, c3) - jnp.minimum(top, c1)
    enclose = outer_w * outer_h
    giou = inter / union - (enclose - union) / enclose
    return weight * (1.0 - giou)


def gelu(value):
    inner = value * (0.7978845608028654 + 0.035677408136300125 * (value * value))
    half = 0.5 * value
    return half + half * jnp.tanh(inner)


def rows_of(index, size):
    return pl.ds(pl.multiple_of(index * size, size), size)


def kernel(
    queries_hbm, features_hbm, cw_hbm, tw_hbm, targets_ref, matches_ref, heads_ref, prior_ref,
    loss_out, query_out, class_out, box_out, side_out,
    feat, feat_t, cw, tw, own_q, all_q, unit_q, exact, inv_norm, units, hidden, raw, side,
    cosine, grads, d_rows, d_emb, small, small_p, small_two, small_z, small_v, small_y, small_vy,
    small_x, small_vx, small_all, q_send, q_recv, g_both, g_recv, s0, s1, r1y, r1x, y2, x2,
    r2x, r2y, t3, r3, fin,
    load_sem, q_ssem, q_rsem, sp_sem, sz_ssem, sz_rsem, sy_ssem, sy_rsem, sx_ssem, sx_rsem,
    sa_ssem, sa_rsem, qs_ssem, qs_rsem, gp_ssem, gp_rsem, y1_ssem, y1_rsem, x1_ssem, x1_rsem,
    x2_ssem, x2_rsem, y2_ssem, y2_rsem, z3_ssem, z3_rsem, f_ssem, f_rsem,
):
    dp = lax.axis_index("dp")
    x = lax.axis_index("group")
    core = dp % NC
    y = (dp // NC) % NY
    z = dp // (NC * NY)

    def at(zz, yy, cc, xx):
        return ((zz * NY + yy) * NC + cc, xx)

    pair = at(z, y, 1 - core, x)
    x_peer = lambda d: at(z, y, core, (x + d) % NX)
    y_peer = lambda d: at(z, (y + d) % NY, core, x)
    z_peer = lambda d: at((z + d) % NZ, y, core, x)
    xs, ys, zs = range(1, NX), range(1, NY), range(1, NZ)

    def remote(src, dst, ssem, rsem, device):
        return pltpu.make_async_remote_copy(
            src_ref=src, dst_ref=dst, send_sem=ssem, recv_sem=rsem,
            device_id=device, device_id_type=MESH,
        )

    loads = [
        pltpu.make_async_copy(queries_hbm, own_q, load_sem.at[0]),
        pltpu.make_async_copy(features_hbm.at[0], feat, load_sem.at[1]),
        pltpu.make_async_copy(cw_hbm, cw, load_sem.at[2]),
        pltpu.make_async_copy(tw_hbm, tw, load_sem.at[3]),
    ]
    for load in loads:
        load.start()

    barrier = pltpu.get_barrier_semaphore()
    peers = [pair] + [x_peer(d) for d in xs] + [y_peer(d) for d in ys] + [z_peer(d) for d in zs]
    for peer in peers:
        pl.semaphore_signal(barrier, inc=1, device_id=peer, device_id_type=MESH)
    loads[0].wait()
    all_q[x] = own_q[...]
    pl.semaphore_wait(barrier, PEERS)

    q_copies = [
        remote(own_q, all_q.at[x], q_ssem.at[d - 1], q_rsem.at[d - 1], x_peer(d)) for d in xs
    ]
    for copy in q_copies:
        copy.start()

    loads[1].wait()
    loads[2].wait()

    def embed(i, carry):
        rows = rows_of(i, BLOCK)
        emb = contract(feat[rows, :], cw[...], 1, 0)
        inv = lax.rsqrt(jnp.sum(emb * emb, axis=1, keepdims=True) + EPSILON)
        unit = emb * inv
        exact[rows, :] = unit
        units[rows, :] = unit.astype(BF16)
        inv_norm[rows, :] = inv
        return carry

    lax.fori_loop(0, ROWS // BLOCK, embed, 0)
    loads[3].wait()

    def box_hidden(i, carry):
        rows = rows_of(i, BLOCK)
        block = feat[rows, :]
        hid = gelu(contract(block, tw[...], 1, 0)).astype(BF16)
        hidden[rows, :] = hid
        raw[:, rows] = contract(heads_ref[...], hid, 1, 1)
        side[:, rows] = contract(heads_ref[...], block, 1, 1)
        feat_t[:, rows] = block.T
        return carry

    lax.fori_loop(0, ROWS // BLOCK, box_hidden, 0)

    matches = matches_ref[...]
    weight = (matches >= 0).astype(F32)
    corners = targets_ref[0].astype(F32) * (1.0 / QUANT)
    terms, pullback = jax.vjp(
        lambda value: box_loss(value, corners, weight), raw[0:4, :] + prior_ref[...]
    )
    d_raw = (GIOU_WEIGHT * pullback(jnp.ones_like(terms))[0]).astype(BF16)
    small[0:4, :] = contract(d_raw, hidden[...], 1, 0)

    for copy in q_copies:
        copy.wait()
    for g in range(NX):
        rows = all_q[g].astype(F32)
        inv = lax.rsqrt(jnp.sum(rows * rows, axis=1, keepdims=True) + EPSILON)
        unit_q[g * QROWS : (g + 1) * QROWS, :] = (rows * inv).astype(BF16)

    step = 32

    def focal(i, loss_sum):
        cols = rows_of(i, BLOCK)
        cosine[...] = contract(unit_q[...], units[cols, :], 1, 1)
        shift = side[4:5, cols] + LOGIT_BIAS
        pre = side[5:6, cols]
        decay = jnp.exp(jnp.minimum(pre, 0.0))
        scale = jnp.where(pre > 0, pre + 1.0, decay)
        match = matches_ref[:, cols]

        def block(j, carry):
            loss, d_shift, d_scale = carry
            rows = rows_of(j, step)
            base = cosine[rows, :] + shift
            index = lax.broadcasted_iota(jnp.int32, (step, BLOCK), 0)
            hit = index == match - j * step
            logit = base * scale
            value = jnp.where(hit, -logit, logit)
            factor = jnp.where(hit, -ALPHA, 1.0 - ALPHA)
            small_exp = jnp.exp(-jnp.abs(value))
            log_one = jnp.log1p(small_exp)
            big = jnp.exp(-log_one)
            little = small_exp * big
            positive = value >= 0
            prob = jnp.where(positive, big, little)
            other = jnp.where(positive, little, big)
            neg_log = jnp.maximum(value, 0.0) + log_one
            square = factor * (prob * prob)
            loss = loss + (jnp.abs(square) * neg_log).reshape(step // 8, 8, BLOCK).sum(0)
            other_log = other * neg_log
            d_logit = square * (prob + (other_log + other_log))
            d_shift = d_shift + d_logit.reshape(step // 8, 8, BLOCK).sum(0)
            d_scale = d_scale + (d_logit * base).reshape(step // 8, 8, BLOCK).sum(0)
            grads[rows, cols] = (d_logit * scale).astype(BF16)
            return loss, d_shift, d_scale

        zero = jnp.zeros((8, BLOCK), F32)
        loss, d_shift, d_scale = lax.fori_loop(0, Q // step, block, (loss_sum, zero, zero))
        d_rows[0:1, cols] = jnp.sum(d_shift, axis=0, keepdims=True)
        d_rows[1:2, cols] = jnp.sum(d_scale, axis=0, keepdims=True) * jnp.where(
            pre > 0, 1.0, decay
        )
        return loss

    focal_sum = lax.fori_loop(0, ROWS // BLOCK, focal, jnp.zeros((8, BLOCK), F32))

    small[4:6, :] = contract(d_rows[...].astype(BF16), feat[...], 1, 0)
    fold = lambda row: row[:, 0:512] + row[:, 512:1024] + row[:, 1024:1536]
    focal_row = jnp.sum(focal_sum, axis=0, keepdims=True)
    small[6:7, 0:512] = GIOU_WEIGHT * fold(terms)
    small[6:7, 0:BLOCK] += focal_row
    small[6:7, 512:1024] = fold(weight)
    small[7:8, :] = jnp.zeros((1, E), F32)
    small_pair = remote(small, small_p, sp_sem.at[0], sp_sem.at[1], pair)
    small_pair.start()

    for n in range(D // BLOCK):
        cols = slice(n * BLOCK, (n + 1) * BLOCK)
        part = contract(grads[...], units[:, cols], 1, 0).astype(BF16)
        for g in range(NX):
            q_send[g, :, cols] = part[g * QROWS : (g + 1) * QROWS, :]
    qs_copies = [
        remote(q_send.at[(x + d) % NX], q_recv.at[d - 1], qs_ssem.at[d - 1], qs_rsem.at[d - 1], x_peer(d))
        for d in xs
    ]
    for copy in qs_copies:
        copy.start()

    small_pair.wait()
    for k in range(NZ):
        lanes = slice(k * 128, (k + 1) * 128)
        small_two[k] = small[:, lanes] + small_p[:, lanes]
    sz_copies = [
        remote(small_two.at[(z + d) % NZ], small_z.at[d - 1], sz_ssem.at[d - 1], sz_rsem.at[d - 1], z_peer(d))
        for d in zs
    ]
    for copy in sz_copies:
        copy.start()

    def embedding_grad(i, carry):
        rows = rows_of(i, BLOCK)
        d_units = contract(grads[:, rows], unit_q[...], 0, 0)
        unit = exact[rows, :]
        along = jnp.sum(unit * d_units, axis=1, keepdims=True)
        d_emb[rows, :] = ((d_units - unit * along) * inv_norm[rows, :]).astype(BF16)
        return carry

    lax.fori_loop(0, ROWS // BLOCK, embedding_grad, 0)

    for copy in sz_copies:
        copy.wait()
    small_v[...] = (
        ((small_two[z] + small_z[0]) + (small_z[1] + small_z[2]))
        + ((small_z[3] + small_z[4]) + (small_z[5] + small_z[6]))
    )
    sy_copies = [
        remote(small_v, small_y.at[d - 1], sy_ssem.at[d - 1], sy_rsem.at[d - 1], y_peer(d)) for d in ys
    ]
    for copy in sy_copies:
        copy.start()

    def pair_copy(j):
        return remote(g_both.at[1 - core, j], g_recv.at[j], gp_ssem.at[j], gp_rsem.at[j], pair)

    def y1_copy(k, j, d):
        return remote(s0.at[(y + d) % NY, k], r1y.at[d - 1, j], y1_ssem.at[d - 1, j], y1_rsem.at[d - 1, j], y_peer(d))

    def x1_copy(d):
        return remote(s1.at[(x + d) % NX], r1x.at[d - 1], x1_ssem.at[d - 1], x1_rsem.at[d - 1], x_peer(d))

    def chunk_of(j):
        return (x + 1 + j) % NX

    def produce(j):
        k = chunk_of(j)
        left = jnp.concatenate(
            [feat_t[rows_of(k, 128), :], feat_t[rows_of(k + NX, 128), :]], axis=0
        )
        for n in range(D // BLOCK):
            cols = slice(n * BLOCK, (n + 1) * BLOCK)
            part = contract(left, d_emb[:, cols], 1, 0).astype(BF16)
            part = part.reshape(2, NY, NC, SHARE, BLOCK)
            for cc in range(NC):
                g_both[cc, j, :, :, :, cols] = part[:, :, cc]

        pair_copy(j).start()

    def consume(j):
        k = chunk_of(j)
        pair_copy(j).wait()
        for h in range(2):
            both = (g_both[core, j, h].astype(F32) + g_recv[j, h].astype(F32)).astype(BF16)
            for yy in range(NY):
                s0[yy, k, h] = both[yy, :, 0:HALF]
                s1[k, yy, h] = both[yy, :, HALF:D]
        for d in ys:
            y1_copy(k, j, d).start()
        if j < NX - 1:
            x1_copy(j + 1).start()

    for j in range(NX):
        produce(j)
        if j > 0:
            consume(j - 1)
        if j == 1:
            for copy in sy_copies:
                copy.wait()
            small_vy[...] = (small_v[...] + small_y[1]) + (small_y[0] + small_y[2])
            sx_copies = [
                remote(small_vy, small_x.at[d - 1], sx_ssem.at[d - 1], sx_rsem.at[d - 1], x_peer(d))
                for d in xs
            ]
            for copy in sx_copies:
                copy.start()
        if j == 3:
            for copy in sx_copies:
                copy.wait()
            small_vx[...] = (small_vy[...] + small_x[1]) + (small_x[0] + small_x[2])
            small_all[z] = small_vx[...]
            sa_copies = [
                remote(small_vx, small_all.at[z], sa_ssem.at[d - 1], sa_rsem.at[d - 1], z_peer(d))
                for d in zs
            ]
            for copy in sa_copies:
                copy.start()
    consume(NX - 1)

    for d in xs:
        x1_copy(d).wait()
    for h in range(2):
        for yy in range(NY):
            total = s1[x, yy, h].astype(F32)
            for d in xs:
                total = total + r1x[d - 1, yy, h].astype(F32)
            x2[yy, h] = total.astype(BF16)
    y2_copies = [
        remote(x2.at[(y + d) % NY], r2y.at[d - 1], y2_ssem.at[d - 1], y2_rsem.at[d - 1], y_peer(d)) for d in ys
    ]
    for copy in y2_copies:
        copy.start()
    x2_copies = []
    for j in range(NX):
        k = chunk_of(j)
        for d in ys:
            y1_copy(k, j, d).wait()
        total = s0[y, k].astype(F32)
        for d in ys:
            total = total + r1y[d - 1, j].astype(F32)
        y2[j] = total.astype(BF16)
        if j < NX - 1:
            copy = remote(y2.at[j], r2x.at[j], x2_ssem.at[j], x2_rsem.at[j], x_peer(j + 1))
            copy.start()
            x2_copies.append(copy)

    for copy in y2_copies:
        copy.wait()
    total = x2[y].astype(F32)
    for d in ys:
        total = total + r2y[d - 1].astype(F32)
    t3[:, 1] = total.astype(BF16)
    for copy in x2_copies:
        copy.wait()
    total = y2[NX - 1].astype(F32)
    for d in xs:
        total = total + r2x[d - 1].astype(F32)
    t3[:, 0] = total.astype(BF16)

    def z3_copy(h):
        distance = (x + NX * h - z + NZ) % NZ
        slot = jnp.maximum(distance - 1, 0)
        return distance, remote(
            t3.at[h], r3.at[slot], z3_ssem.at[h], z3_rsem.at[slot], z_peer(distance)
        )

    for h in range(2):
        distance, copy = z3_copy(h)
        pl.when(distance != 0)(copy.start)

    for copy in sa_copies:
        copy.wait()
    for k in range(NZ):
        small[:, k * 128 : (k + 1) * 128] = small_all[k]
    per = 1.0 / jnp.sum(small[6:7, 512:1024], axis=1, keepdims=True)
    box_out[...] = small[0:4, :] * per
    side_out[...] = small[4:6, :] * per
    loss_out[...] = jnp.sum(small[6:7, 0:512], axis=1, keepdims=True) * per

    for copy in qs_copies:
        copy.wait()
    sums = q_send[x].astype(F32)
    for d in xs:
        sums = sums + q_recv[d - 1].astype(F32)
    mine = own_q[...].astype(F32)
    inv = lax.rsqrt(jnp.sum(mine * mine, axis=1, keepdims=True) + EPSILON)
    mine = mine * inv
    along = jnp.sum(mine * sums, axis=1, keepdims=True)
    query_out[...] = (sums - mine * along) * (inv * per)

    owner = x == z % NX
    f_copies = [remote(fin, fin, f_ssem.at[d - 1], f_rsem.at[0], x_peer(d)) for d in xs]

    @pl.when(owner)
    def _():
        total = t3[z // NX].astype(F32)
        for d in zs:
            remote(t3.at[0], r3.at[d - 1], z3_ssem.at[0], z3_rsem.at[d - 1], z_peer(d)).wait_recv()
            total = total + r3[d - 1].astype(F32)
        fin[...] = total
        for copy in f_copies:
            copy.start()
        for copy in f_copies:
            copy.wait_send()

    @pl.when(jnp.logical_not(owner))
    def _():
        f_copies[0].wait_recv()

    for h in range(2):
        distance, copy = z3_copy(h)
        pl.when(distance != 0)(copy.wait_send)
    class_out[:, 0:HALF] = fin[0] * per
    class_out[:, HALF:D] = fin[1] * per


def on_device(features, targets, matches, queries, class_weight, trunk_weight, head_rows):
    hbm = pl.BlockSpec(memory_space=pl.ANY)
    vmem = pl.BlockSpec(memory_space=pltpu.VMEM)
    dma = lambda *shape: pltpu.SemaphoreType.DMA(shape)
    buf = lambda kind, *shape: pltpu.VMEM(shape, kind)
    loss, query, classes, box, side = pl.pallas_call(
        kernel,
        out_shape=(
            jax.ShapeDtypeStruct((1, 1), F32),
            jax.ShapeDtypeStruct((QROWS, D), F32),
            jax.ShapeDtypeStruct((SHARE, D), F32),
            jax.ShapeDtypeStruct((4, E), F32),
            jax.ShapeDtypeStruct((2, E), F32),
        ),
        in_specs=[hbm] * 4 + [vmem] * 4,
        out_specs=[vmem] * 5,
        scratch_shapes=[
            buf(BF16, ROWS, E),
            buf(BF16, E, ROWS),
            buf(BF16, E, D),
            buf(BF16, E, E),
            buf(BF16, QROWS, D),
            buf(BF16, NX, QROWS, D),
            buf(BF16, Q, D),
            buf(F32, ROWS, D),
            buf(F32, ROWS, 1),
            buf(BF16, ROWS, D),
            buf(BF16, ROWS, E),
            buf(F32, 6, ROWS),
            buf(F32, 6, ROWS),
            buf(F32, Q, BLOCK),
            buf(BF16, Q, ROWS),
            buf(F32, 2, ROWS),
            buf(BF16, ROWS, D),
            buf(F32, 8, E),
            buf(F32, 8, E),
            buf(F32, NZ, 8, 128),
            buf(F32, NZ - 1, 8, 128),
            buf(F32, 8, 128),
            buf(F32, NY - 1, 8, 128),
            buf(F32, 8, 128),
            buf(F32, NX - 1, 8, 128),
            buf(F32, 8, 128),
            buf(F32, NZ, 8, 128),
            buf(BF16, NX, QROWS, D),
            buf(BF16, NX - 1, QROWS, D),
            buf(BF16, NC, NX, 2, NY, SHARE, D),
            buf(BF16, NX, 2, NY, SHARE, D),
            buf(BF16, NY, NX, 2, SHARE, HALF),
            buf(BF16, NX, NY, 2, SHARE, HALF),
            buf(BF16, NY - 1, NX, 2, SHARE, HALF),
            buf(BF16, NX - 1, NY, 2, SHARE, HALF),
            buf(BF16, NX, 2, SHARE, HALF),
            buf(BF16, NY, 2, SHARE, HALF),
            buf(BF16, NX - 1, 2, SHARE, HALF),
            buf(BF16, NY - 1, 2, SHARE, HALF),
            buf(BF16, 2, 2, SHARE, HALF),
            buf(BF16, NZ - 1, 2, SHARE, HALF),
            buf(F32, 2, SHARE, HALF),
            dma(4), dma(NX - 1), dma(NX - 1), dma(2),
            dma(NZ - 1), dma(NZ - 1), dma(NY - 1), dma(NY - 1), dma(NX - 1), dma(NX - 1),
            dma(NZ - 1), dma(NZ - 1), dma(NX - 1), dma(NX - 1), dma(NX), dma(NX),
            dma(NY - 1, NX), dma(NY - 1, NX), dma(NX - 1), dma(NX - 1),
            dma(NX - 1), dma(NX - 1), dma(NY - 1), dma(NY - 1),
            dma(2), dma(NZ - 1), dma(NX - 1), dma(1),
        ],
        compiler_params=pltpu.CompilerParams(
            collective_id=0, has_side_effects=True, vmem_limit_bytes=56 * 1024 * 1024
        ),
        cost_estimate=pl.CostEstimate(
            flops=11_000_000_000, bytes_accessed=8_000_000, transcendentals=4_000_000
        ),
    )(
        queries, features, class_weight, trunk_weight, targets, matches, head_rows,
        jnp.asarray(box_prior(ROWS)),
    )
    return loss[0, 0], query, classes, box, side


def solution(mesh):
    in_specs = (
        P(("dp", "group"), None, None),
        P(("dp", "group"), None, None),
        P(("dp", "group"), None),
        P(("dp", "group"), None),
        P(),
        P(),
        P(),
    )
    out_specs = (P(), P(("dp", "group"), None), P("dp", None), P(), P())
    return jax.shard_map(
        on_device, mesh=mesh, in_specs=in_specs, out_specs=out_specs, check_vma=False
    )
```

time: 334 us -> 67.9 us (0.20)
  waiting for transfers between devices: 170 us -> 0 us
  blocking collectives: 94 us -> 0 us
  Pallas kernels: 0 us -> 58.9 us
  matrix products: 36.7 us -> 0 us
  between operations: 18.8 us -> 2.39 us
  other arithmetic: 10.4 us -> 0 us
    psum x1 -> x0, waiting for transfers between devices: 170 us -> none  [on_device(): lax.psum(contract(features_one, d_embedding, 0, 0), ('dp', 'group'))]
    psum x1 -> x0, blocking collectives: 79.5 us -> none  [on_device(): lax.psum((focal_local, giou_local, small_local), ('dp', 'group'))]
    pallas_call x0 -> x1, Pallas kernels: none -> 58.9 us  [on_device(): pl.pallas_call(kernel, out_shape=(jax.ShapeDtypeStruct((1, 1), F32), jax....]
    dot_general x10 -> x0, matrix products: 36.7 us -> none  [the longest x7 21.3 us: contract(): lax.dot_general(left, right, (((left_dim,), (right_dim,)), ((), ())), pre...]
    all_gather x1 -> x0, blocking collectives: 14.5 us -> none  [on_device(): group_queries = lax.all_gather(unit_queries, 'group', axis=0, tiled=True)]
    div x5 -> x0, other arithmetic: 6.11 us -> none  [the longest x1 1.81 us: on_device(): class_part / positives]
  transfers between devices with their start and end apart: 2 -> 0, of which waited for: 1 -> 0; matrix products, arithmetic and copies ran while one was open for 8% -> 0% of each run, Pallas kernels for 0% -> 0%
where the time goes in v1:
time: 67.9 us; the launch traced here: 67 us
  Pallas kernels  58.9 us (87%)
  local copies, waits for them, and re-layouts  5.73 us (8%)
  between operations  2.39 us (4%)
    pallas_call x1, Pallas kernels, on_device(): pl.pallas_call(kernel, out_shape=(jax.ShapeDtypeStruct((1, 1), F32), jax....  58.9 us
    unnamed x4, local copies, waits for them, and re-layouts  5.73 us

profile of v1, /device:TPU:2, one launch (start us, length us, event | category | flops | bytes accessed | tf_op | source)
XLA Modules:
  0.0 67.0 jit_solution(13031169328533063405)
XLA Ops:
  0.6 58.9 %shard_map.119 = (f32[1,1]{1,0:T(1,128)}, f32[96,768]{1,0:T(8,128)}, f32[16,768]{1,0:T(8,128)}, f32[4,1024]{1,0:T(4,128)}, f32[2,1024]{1,0:T(2,128)}) custom-call(bf16[96,768]{1,0:T(8,128)(2,1)} %queries_hbm.1, bf16[1,1536,1024]{2,1,0:T(8,128)(2,1)} %features_hbm.1, bf16[1024,768]{1,0:T(8,128)(2,1)} %cw_hbm.1, bf16[1024,1024]{1,0:T(8,128)(2,1)} %tw_hbm.1, ...), custom_call_target="tpu_custom_call" | custom-call | flops 11000000512 | bytes 8000000 | tf_op jit(solution)/shard_map/pallas_call | solution.py:447
  60.2 1.7 %copy.19 = f32[96,768]{1,0:T(8,128)} copy(f32[96,768]{1,0:T(8,128)} %get-tuple-element.21) | data formatting | bytes 589824
  61.9 1.4 %copy.20 = f32[16,768]{1,0:T(8,128)} copy(f32[16,768]{1,0:T(8,128)} %get-tuple-element.22) | data formatting | bytes 98304
  63.3 1.3 %copy.21 = f32[4,1024]{1,0:T(4,128)} copy(f32[4,1024]{1,0:T(4,128)} %get-tuple-element.23) | data formatting | bytes 32768
  64.6 1.3 %copy.22 = f32[2,1024]{1,0:T(2,128)} copy(f32[2,1024]{1,0:T(2,128)} %get-tuple-element.24) | data formatting | bytes 16384

commit v2 on v1

v2 whole, which is shorter than its diff:
```python
import functools

import jax
import jax.numpy as jnp
import numpy as np
from jax import lax
from jax.experimental import pallas as pl
from jax.experimental.pallas import tpu as pltpu
from jax.sharding import PartitionSpec as P

MESH = pl.DeviceIdType.MESH
F32 = jnp.float32
BF16 = jnp.bfloat16

GRID = 72
QUANT = 1024
ALPHA = 0.25
GIOU_WEIGHT = 2.0
LOGIT_BIAS = -4.0
EPSILON = 1e-06

NX, NY, NZ, NC = 4, 4, 8, 2
E, D, ROWS, Q = 1024, 768, 1536, 384
QROWS = Q // NX
SHARE = E // (NZ * NY * NC)
HALF = D // 2
BLOCK = 768
TILE = 256
PEERS = 1 + (NX * NY - 1) + (NZ - 1)


def contract(left, right, left_dim, right_dim):
    return lax.dot_general(
        left, right, (((left_dim,), (right_dim,)), ((), ())), preferred_element_type=F32
    )


def box_prior(length):
    index = np.arange(length)

    def logit(value):
        return np.log(value) - np.log1p(-value)

    across = logit((index % GRID + 0.5) / GRID)
    down = logit((index // GRID + 0.5) / GRID)
    size = np.full((length,), logit(1.0 / GRID))
    return np.stack([across, down, size, size], 0).astype(np.float32)


def box_loss(box_raw, corners, weight):
    box = jax.nn.sigmoid(box_raw)
    cx, cy, bw, bh = (box[i : i + 1] for i in range(4))
    c0, c1, c2, c3 = (corners[i : i + 1] for i in range(4))
    left = cx - 0.5 * bw
    right = cx + 0.5 * bw
    top = cy - 0.5 * bh
    bottom = cy + 0.5 * bh
    inter_w = jnp.maximum(jnp.minimum(right, c2) - jnp.maximum(left, c0), 0.0)
    inter_h = jnp.maximum(jnp.minimum(bottom, c3) - jnp.maximum(top, c1), 0.0)
    inter = inter_w * inter_h
    union = bw * bh + (c2 - c0) * (c3 - c1) - inter
    outer_w = jnp.maximum(right, c2) - jnp.minimum(left, c0)
    outer_h = jnp.maximum(bottom, c3) - jnp.minimum(top, c1)
    enclose = outer_w * outer_h
    giou = inter / union - (enclose - union) / enclose
    return weight * (1.0 - giou)


def gelu(value):
    inner = value * (0.7978845608028654 + 0.035677408136300125 * (value * value))
    half = 0.5 * value
    return half + half * jnp.tanh(inner)


def rows_of(index, size):
    return pl.ds(pl.multiple_of(index * size, size), size)


def kernel(
    queries_hbm, features_hbm, cw_hbm, tw_hbm, targets_ref, matches_ref, heads_ref, prior_ref,
    loss_out, query_out, class_out, box_out, side_out,
    feat, cw, tw, own_q, all_q, unit_q, exact, inv_norm, units, hidden, raw, side,
    cosine, grads, d_rows, d_emb, small, small_p, small_two, small_z, small_v, small_xy, small_sum,
    small_all, q_send, q_recv, g_both, g_recv, s0, s1, r1y, r1x, t0, t1, r2a, r2b, u0, u1, r3a, r3b,
    load_sem, q_ssem, q_rsem, sp_sem, sz_ssem, sz_rsem, sxy_ssem, sxy_rsem,
    sa_ssem, sa_rsem, qs_ssem, qs_rsem, gp_ssem, gp_rsem, y1_ssem, y1_rsem, x1_ssem, x1_rsem,
    z0_ssem, z0_rsem, z1_ssem, z1_rsem, f0_ssem, f0_rsem, f1_ssem, f1_rsem,
):
    dp = lax.axis_index("dp")
    x = lax.axis_index("group")
    core = dp % NC
    y = (dp // NC) % NY
    z = dp // (NC * NY)

    def at(zz, yy, cc, xx):
        return ((zz * NY + yy) * NC + cc, xx)

    pair = at(z, y, 1 - core, x)
    x_peer = lambda d: at(z, y, core, (x + d) % NX)
    y_peer = lambda d: at(z, (y + d) % NY, core, x)
    xy_peer = lambda dy, dx: at(z, (y + dy) % NY, core, (x + dx) % NX)
    z_peer = lambda d: at((z + d) % NZ, y, core, x)
    xs, ys, zs = range(1, NX), range(1, NY), range(1, NZ)
    plane = [(dy, dx) for dy in range(NY) for dx in range(NX) if dy or dx]

    def remote(src, dst, ssem, rsem, device):
        return pltpu.make_async_remote_copy(
            src_ref=src, dst_ref=dst, send_sem=ssem, recv_sem=rsem,
            device_id=device, device_id_type=MESH,
        )

    loads = [
        pltpu.make_async_copy(queries_hbm, own_q, load_sem.at[0]),
        pltpu.make_async_copy(features_hbm.at[0], feat, load_sem.at[1]),
        pltpu.make_async_copy(cw_hbm, cw, load_sem.at[2]),
        pltpu.make_async_copy(tw_hbm, tw, load_sem.at[3]),
    ]
    for load in loads:
        load.start()

    barrier = pltpu.get_barrier_semaphore()
    peers = [pair] + [xy_peer(dy, dx) for dy, dx in plane] + [z_peer(d) for d in zs]
    for peer in peers:
        pl.semaphore_signal(barrier, inc=1, device_id=peer, device_id_type=MESH)
    loads[0].wait()
    all_q[x] = own_q[...]
    loads[1].wait()
    loads[2].wait()

    def embed(i, carry):
        rows = rows_of(i, BLOCK)
        emb = contract(feat[rows, :], cw[...], 1, 0)
        inv = lax.rsqrt(jnp.sum(emb * emb, axis=1, keepdims=True) + EPSILON)
        unit = emb * inv
        exact[rows, :] = unit
        units[rows, :] = unit.astype(BF16)
        inv_norm[rows, :] = inv
        return carry

    embed(0, 0)

    pl.semaphore_wait(barrier, PEERS)
    q_copies = [
        remote(own_q, all_q.at[x], q_ssem.at[d - 1], q_rsem.at[d - 1], x_peer(d)) for d in (1, 3, 2)
    ]
    for copy in q_copies:
        copy.start()
    embed(1, 0)
    loads[3].wait()

    def box_hidden(i, carry):
        rows = rows_of(i, BLOCK)
        block = feat[rows, :]
        hid = gelu(contract(block, tw[...], 1, 0)).astype(BF16)
        hidden[rows, :] = hid
        raw[:, rows] = contract(hid, heads_ref[...], 1, 1).T
        side[:, rows] = contract(block, heads_ref[...], 1, 1).T
        return carry

    lax.fori_loop(0, ROWS // BLOCK, box_hidden, 0)

    matches = matches_ref[...]
    weight = (matches >= 0).astype(F32)
    corners = targets_ref[0].astype(F32) * (1.0 / QUANT)
    terms, pullback = jax.vjp(
        lambda value: box_loss(value, corners, weight), raw[0:4, :] + prior_ref[...]
    )
    d_raw = (GIOU_WEIGHT * pullback(jnp.ones_like(terms))[0]).astype(BF16)
    small[0:4, :] = contract(d_raw, hidden[...], 1, 0)

    for copy in q_copies:
        copy.wait()
    for g in range(NX):
        rows = all_q[g].astype(F32)
        inv = lax.rsqrt(jnp.sum(rows * rows, axis=1, keepdims=True) + EPSILON)
        unit_q[g * QROWS : (g + 1) * QROWS, :] = (rows * inv).astype(BF16)

    step = 32

    def focal(i, loss_sum):
        cosine[...] = contract(unit_q[...], units[rows_of(i, BLOCK), :], 1, 1)

        def tile(n, loss_sum):
            cols = rows_of(i * (BLOCK // TILE) + n, TILE)
            here = rows_of(n, TILE)
            shift = side[4:5, cols] + LOGIT_BIAS
            pre = side[5:6, cols]
            decay = jnp.exp(jnp.minimum(pre, 0.0))
            scale = jnp.where(pre > 0, pre + 1.0, decay)
            match = matches_ref[:, cols]

            def block(j, carry):
                loss, d_shift, d_scale = carry
                rows = rows_of(j, step)
                base = cosine[rows, here] + shift
                index = lax.broadcasted_iota(jnp.int32, (step, TILE), 0)
                hit = index == match - j * step
                logit = base * scale
                value = jnp.where(hit, -logit, logit)
                factor = jnp.where(hit, -ALPHA, 1.0 - ALPHA)
                small_exp = jnp.exp(-jnp.abs(value))
                log_one = jnp.log1p(small_exp)
                big = jnp.exp(-log_one)
                little = small_exp * big
                positive = value >= 0
                prob = jnp.where(positive, big, little)
                other = jnp.where(positive, little, big)
                neg_log = jnp.maximum(value, 0.0) + log_one
                square = factor * (prob * prob)
                loss = loss + (jnp.abs(square) * neg_log).reshape(step // 8, 8, TILE).sum(0)
                other_log = other * neg_log
                d_logit = square * (prob + (other_log + other_log))
                d_shift = d_shift + d_logit.reshape(step // 8, 8, TILE).sum(0)
                d_scale = d_scale + (d_logit * base).reshape(step // 8, 8, TILE).sum(0)
                grads[rows, cols] = (d_logit * scale).astype(BF16)
                return loss, d_shift, d_scale

            zero = jnp.zeros((8, TILE), F32)
            loss, d_shift, d_scale = lax.fori_loop(0, Q // step, block, (loss_sum, zero, zero))
            d_rows[0:1, cols] = jnp.sum(d_shift, axis=0, keepdims=True)
            d_rows[1:2, cols] = jnp.sum(d_scale, axis=0, keepdims=True) * jnp.where(
                pre > 0, 1.0, decay
            )
            return loss

        return lax.fori_loop(0, BLOCK // TILE, tile, loss_sum)

    focal_sum = lax.fori_loop(0, ROWS // BLOCK, focal, jnp.zeros((8, TILE), F32))

    def embedding_grad(i, carry):
        rows = rows_of(i, BLOCK)
        d_units = contract(grads[:, rows], unit_q[...], 0, 0)
        unit = exact[rows, :]
        along = jnp.sum(unit * d_units, axis=1, keepdims=True)
        d_emb[rows, :] = ((d_units - unit * along) * inv_norm[rows, :]).astype(BF16)
        return carry

    lax.fori_loop(0, ROWS // BLOCK, embedding_grad, 0)

    def pair_copy(k):
        return remote(g_both.at[1 - core, k], g_recv.at[k], gp_ssem.at[k], gp_rsem.at[k], pair)

    def y1_copy(k, d):
        return remote(s0.at[(y + d) % NY, k], r1y.at[d - 1, k], y1_ssem.at[d - 1, k], y1_rsem.at[d - 1, k], y_peer(d))

    def x1_copy(k, d):
        return remote(s1.at[(x + d) % NX, k], r1x.at[d - 1, k], x1_ssem.at[d - 1, k], x1_rsem.at[d - 1, k], x_peer(d))

    def z_copy(half, k, h):
        distance = (k + NX * h - z + NZ) % NZ
        slot = jnp.maximum(distance - 1, 0)
        source, target, ssem, rsem = ((t0, r2a, z0_ssem, z0_rsem), (t1, r2b, z1_ssem, z1_rsem))[half]
        return distance, remote(
            source.at[k, h], target.at[slot], ssem.at[k, h], rsem.at[slot], z_peer(distance)
        )

    def produce(k):
        left = jnp.concatenate(
            [feat[:, k * 128 : (k + 1) * 128], feat[:, (k + NX) * 128 : (k + NX + 1) * 128]], axis=1
        )
        part = contract(left, d_emb[...], 0, 0).astype(BF16).reshape(2, NY, NC, SHARE, D)
        for cc in range(NC):
            g_both[cc, k] = part[:, :, cc]
        pair_copy(k).start()

    def consume(k):
        pair_copy(k).wait_recv()
        for h in range(2):
            both = (g_both[core, k, h].astype(F32) + g_recv[k, h].astype(F32)).astype(BF16)
            for yy in range(NY):
                s0[yy, k, h] = both[yy, :, 0:HALF]
                s1[yy, k, h] = both[yy, :, HALF:D]
        for d in ys:
            y1_copy(k, d).start()
        for d in xs:
            x1_copy(k, d).start()

    def forward(k):
        for half in range(2):
            own, got, copy, mine = ((s0, r1y, y1_copy, y), (s1, r1x, x1_copy, x))[half]
            total = own[mine, k].astype(F32)
            for d in ys:
                copy(k, d).wait_recv()
                total = total + got[d - 1, k].astype(F32)
            (t0, t1)[half][k] = total.astype(BF16)
            for h in range(2):
                distance, move = z_copy(half, k, h)
                pl.when(distance != 0)(move.start)

    produce(0)
    produce(1)
    consume(0)
    produce(2)
    consume(1)
    produce(3)
    consume(2)

    for n in range(D // TILE):
        cols = slice(n * TILE, (n + 1) * TILE)
        part = contract(grads[...], units[:, cols], 1, 0).astype(BF16)
        for g in range(NX):
            q_send[g, :, cols] = part[g * QROWS : (g + 1) * QROWS, :]
    consume(3)
    qs_copies = [
        remote(q_send.at[(x + d) % NX], q_recv.at[d - 1], qs_ssem.at[d - 1], qs_rsem.at[d - 1], x_peer(d))
        for d in xs
    ]
    for copy in qs_copies:
        copy.start()

    small[4:6, :] = contract(d_rows[...].astype(BF16), feat[...], 1, 0)
    fold = lambda row: row[:, 0:512] + row[:, 512:1024] + row[:, 1024:1536]
    focal_row = jnp.sum(focal_sum, axis=0, keepdims=True)
    small[6:7, 0:512] = GIOU_WEIGHT * fold(terms)
    small[6:7, 0:TILE] += focal_row
    small[6:7, 512:1024] = fold(weight)
    small[7:8, :] = jnp.zeros((1, E), F32)
    small_pair = remote(small, small_p, sp_sem.at[0], sp_sem.at[1], pair)
    small_pair.start()

    forward(0)
    small_pair.wait()
    for k in range(NZ):
        lanes = slice(k * 128, (k + 1) * 128)
        small_two[k] = small[:, lanes] + small_p[:, lanes]
    sz_copies = [
        remote(small_two.at[(z + d) % NZ], small_z.at[d - 1], sz_ssem.at[d - 1], sz_rsem.at[d - 1], z_peer(d))
        for d in zs
    ]
    for copy in sz_copies:
        copy.start()
    for k in range(1, NX):
        forward(k)

    for copy in sz_copies:
        copy.wait_recv()
    small_v[...] = (
        ((small_two[z] + small_z[0]) + (small_z[1] + small_z[2]))
        + ((small_z[3] + small_z[4]) + (small_z[5] + small_z[6]))
    )
    sxy_copies = [
        remote(small_v, small_xy.at[dy, dx], sxy_ssem.at[dy, dx], sxy_rsem.at[dy, dx], xy_peer(dy, dx))
        for dy, dx in plane
    ]
    for copy in sxy_copies:
        copy.start()

    def over_z(total, got, half):
        for d in zs:
            remote(t0.at[0, 0], got.at[d - 1], z0_ssem.at[0, 0], (z0_rsem, z1_rsem)[half].at[d - 1], z_peer(d)).wait_recv()
            total = total + got[d - 1].astype(F32)
        return total.astype(BF16)

    u0[...] = over_z(t0[z % NX, z // NX].astype(F32), r2a, 0)
    f0_copies = [remote(u0, r3a.at[d - 1], f0_ssem.at[d - 1], f0_rsem.at[d - 1], x_peer(d)) for d in xs]
    for copy in f0_copies:
        copy.start()
    u1[...] = over_z(t1[z % NX, z // NX].astype(F32), r2b, 1)

    def f1_copy(target):
        return remote(u1, r3b.at[y], f1_ssem.at[target], f1_rsem.at[y], at(z, x, core, target))

    for target in range(NX):
        itself = jnp.logical_and(y == x, x == target)
        pl.when(jnp.logical_not(itself))(f1_copy(target).start)

    @pl.when(y == x)
    def _():
        r3b[y] = u1[...]

    for copy in sxy_copies:
        copy.wait_recv()
    small_xy[0, 0] = small_v[...]
    line = [
        (small_xy[dy, 0] + small_xy[dy, 2]) + (small_xy[dy, 1] + small_xy[dy, 3]) for dy in range(NY)
    ]
    small_sum[...] = (line[0] + line[2]) + (line[1] + line[3])
    small_all[z] = small_sum[...]
    sa_copies = [
        remote(small_sum, small_all.at[z], sa_ssem.at[d - 1], sa_rsem.at[d - 1], z_peer(d)) for d in zs
    ]
    for copy in sa_copies:
        copy.start()

    for copy in qs_copies:
        copy.wait_recv()
    sums = q_send[x].astype(F32)
    for d in xs:
        sums = sums + q_recv[d - 1].astype(F32)
    mine = own_q[...].astype(F32)
    inv = lax.rsqrt(jnp.sum(mine * mine, axis=1, keepdims=True) + EPSILON)
    mine = mine * inv
    along = jnp.sum(mine * sums, axis=1, keepdims=True)
    query_raw = (sums - mine * along) * inv

    for copy in sa_copies:
        copy.wait_recv()
    for k in range(NZ):
        small[:, k * 128 : (k + 1) * 128] = small_all[k]
    per = 1.0 / jnp.sum(small[6:7, 512:1024], axis=1, keepdims=True)
    box_out[...] = small[0:4, :] * per
    side_out[...] = small[4:6, :] * per
    loss_out[...] = jnp.sum(small[6:7, 0:512], axis=1, keepdims=True) * per
    query_out[...] = query_raw * per

    for copy in f0_copies:
        copy.wait_recv()
    total = (u0[...].astype(F32) + r3a[1].astype(F32)) + (r3a[0].astype(F32) + r3a[2].astype(F32))
    class_out[:, 0:HALF] = total * per
    for source in range(NY):
        itself = jnp.logical_and(y == x, y == source)
        arrived = remote(u1, r3b.at[source], f1_ssem.at[0], f1_rsem.at[source], at(z, source, core, y))
        pl.when(jnp.logical_not(itself))(arrived.wait_recv)
    total = r3b[0].astype(F32)
    for source in range(1, NY):
        total = total + r3b[source].astype(F32)
    class_out[:, HALF:D] = total * per

    for k in range(NX):
        pair_copy(k).wait_send()
        for d in ys:
            y1_copy(k, d).wait_send()
            x1_copy(k, d).wait_send()
        for half in range(2):
            for h in range(2):
                distance, move = z_copy(half, k, h)
                pl.when(distance != 0)(move.wait_send)
    for copy in qs_copies + sz_copies + sxy_copies + sa_copies + f0_copies:
        copy.wait_send()
    for target in range(NX):
        itself = jnp.logical_and(y == x, x == target)
        pl.when(jnp.logical_not(itself))(f1_copy(target).wait_send)


def finish(*refs):
    count = len(refs) // 2
    for i in range(count):
        refs[count + i][...] = refs[i][...]


def on_device(features, targets, matches, queries, class_weight, trunk_weight, head_rows):
    hbm = pl.BlockSpec(memory_space=pl.ANY)
    vmem = pl.BlockSpec(memory_space=pltpu.VMEM)
    dma = lambda *shape: pltpu.SemaphoreType.DMA(shape)
    buf = lambda kind, *shape: pltpu.VMEM(shape, kind)
    loss, query, classes, box, side = pl.pallas_call(
        kernel,
        out_shape=(
            jax.ShapeDtypeStruct((1, 1), F32),
            jax.ShapeDtypeStruct((QROWS, D), F32),
            jax.ShapeDtypeStruct((SHARE, D), F32),
            jax.ShapeDtypeStruct((4, E), F32),
            jax.ShapeDtypeStruct((2, E), F32),
        ),
        in_specs=[hbm] * 4 + [vmem] * 4,
        out_specs=[vmem] * 5,
        scratch_shapes=[
            buf(BF16, ROWS, E),
            buf(BF16, E, D),
            buf(BF16, E, E),
            buf(BF16, QROWS, D),
            buf(BF16, NX, QROWS, D),
            buf(BF16, Q, D),
            buf(F32, ROWS, D),
            buf(F32, ROWS, 1),
            buf(BF16, ROWS, D),
            buf(BF16, ROWS, E),
            buf(F32, 6, ROWS),
            buf(F32, 6, ROWS),
            buf(F32, Q, BLOCK),
            buf(BF16, Q, ROWS),
            buf(F32, 2, ROWS),
            buf(BF16, ROWS, D),
            buf(F32, 8, E),
            buf(F32, 8, E),
            buf(F32, NZ, 8, 128),
            buf(F32, NZ - 1, 8, 128),
            buf(F32, 8, 128),
            buf(F32, NY, NX, 8, 128),
            buf(F32, 8, 128),
            buf(F32, NZ, 8, 128),
            buf(BF16, NX, QROWS, D),
            buf(BF16, NX - 1, QROWS, D),
            buf(BF16, NC, NX, 2, NY, SHARE, D),
            buf(BF16, NX, 2, NY, SHARE, D),
            buf(BF16, NY, NX, 2, SHARE, HALF),
            buf(BF16, NY, NX, 2, SHARE, HALF),
            buf(BF16, NY - 1, NX, 2, SHARE, HALF),
            buf(BF16, NX - 1, NX, 2, SHARE, HALF),
            buf(BF16, NX, 2, SHARE, HALF),
            buf(BF16, NX, 2, SHARE, HALF),
            buf(BF16, NZ - 1, SHARE, HALF),
            buf(BF16, NZ - 1, SHARE, HALF),
            buf(BF16, SHARE, HALF),
            buf(BF16, SHARE, HALF),
            buf(BF16, NX - 1, SHARE, HALF),
            buf(BF16, NY, SHARE, HALF),
            dma(4), dma(NX - 1), dma(NX - 1), dma(2),
            dma(NZ - 1), dma(NZ - 1), dma(NY, NX), dma(NY, NX),
            dma(NZ - 1), dma(NZ - 1), dma(NX - 1), dma(NX - 1), dma(NX), dma(NX),
            dma(NY - 1, NX), dma(NY - 1, NX), dma(NX - 1, NX), dma(NX - 1, NX),
            dma(NX, 2), dma(NZ - 1), dma(NX, 2), dma(NZ - 1),
            dma(NX - 1), dma(NX - 1), dma(NX), dma(NY),
        ],
        compiler_params=pltpu.CompilerParams(
            collective_id=0, has_side_effects=True, vmem_limit_bytes=56 * 1024 * 1024
        ),
        cost_estimate=pl.CostEstimate(
            flops=11_000_000_000, bytes_accessed=8_000_000, transcendentals=4_000_000
        ),
    )(
        queries, features, class_weight, trunk_weight, targets, matches, head_rows,
        jnp.asarray(box_prior(ROWS)),
    )
    results = (loss, query, classes, box, side)
    loss, query, classes, box, side = pl.pallas_call(
        finish,
        out_shape=tuple(jax.ShapeDtypeStruct(r.shape, F32) for r in results),
        in_specs=[vmem] * 5,
        out_specs=[vmem] * 5,
    )(*results)
    return loss[0, 0], query, classes, box, side


def solution(mesh):
    in_specs = (
        P(("dp", "group"), None, None),
        P(("dp", "group"), None, None),
        P(("dp", "group"), None),
        P(("dp", "group"), None),
        P(),
        P(),
        P(),
    )
    out_specs = (P(), P(("dp", "group"), None), P("dp", None), P(), P())
    return jax.shard_map(
        on_device, mesh=mesh, in_specs=in_specs, out_specs=out_specs, check_vma=False
    )
```

time: 67.9 us -> 57 us (0.84); the launches traced: 67 us -> 56.8 us
  local copies, waits for them, and re-layouts: 5.73 us -> 0 us
  Pallas kernels: 58.9 us -> 56.2 us
  between operations: 2.39 us -> 0.64 us
    unnamed x4 -> x0, local copies, waits for them, and re-layouts: 5.73 us -> none
    pallas_call x1, Pallas kernels: 58.9 us -> 53.8 us  [on_device(): pl.pallas_call(kernel, out_shape=(jax.ShapeDtypeStruct((1, 1), F32), jax....]
    pallas_call x0 -> x1, Pallas kernels: none -> 2.37 us  [on_device(): pl.pallas_call(finish, out_shape=tuple((jax.ShapeDtypeStruct(r.shape, F32...]
where the time goes in v2:
time: 57 us; the launch traced here: 56.8 us
  Pallas kernels  56.2 us (99%)
  between operations  0.64 us (1%)
    pallas_call x1, Pallas kernels, on_device(): pl.pallas_call(kernel, out_shape=(jax.ShapeDtypeStruct((1, 1), F32), jax....  53.8 us
    pallas_call x1, Pallas kernels, on_device(): pl.pallas_call(finish, out_shape=tuple((jax.ShapeDtypeStruct(r.shape, F32...  2.37 us

profile of v2, /device:TPU:2, one launch (start us, length us, event | category | flops | bytes accessed | tf_op | source)
XLA Modules:
  0.0 56.8 jit_solution(1941161525767591191)
XLA Ops:
  0.6 53.8 %shard_map.119 = (f32[1,1]{1,0:T(1,128)}, f32[96,768]{1,0:T(8,128)}, f32[16,768]{1,0:T(8,128)}, f32[4,1024]{1,0:T(4,128)}, f32[2,1024]{1,0:T(2,128)}) custom-call(bf16[96,768]{1,0:T(8,128)(2,1)} %queries_hbm.1, bf16[1,1536,1024]{2,1,0:T(8,128)(2,1)} %features_hbm.1, bf16[1024,768]{1,0:T(8,128)(2,1)} %cw_hbm.1, bf16[1024,1024]{1,0:T(8,128)(2,1)} %tw_hbm.1, ...), custom_call_target="tpu_custom_call" | custom-call | flops 11000000512 | bytes 8000000 | tf_op jit(solution)/shard_map/pallas_call | solution.py:446
  54.4 2.4 %shard_map.120 = (f32[1,1]{1,0:T(1,128)}, f32[96,768]{1,0:T(8,128)}, f32[16,768]{1,0:T(8,128)}, f32[4,1024]{1,0:T(4,128)}, f32[2,1024]{1,0:T(2,128)}) custom-call(f32[1,1]{1,0:T(1,128)} %get-tuple-element.15.refs_0_, f32[96,768]{1,0:T(8,128)} %get-tuple-element.16.refs_1_, f32[16,768]{1,0:T(8,128)} %get-tuple-element.17.refs_2_, ...), custom_call_target="tpu_custom_call" | custom-call | tf_op jit(solution)/shard_map/pallas_call | solution.py:516

commit v3 on v2

--- a/solution.py
+++ b/solution.py
@@ -18,6 +18,7 @@
 GIOU_WEIGHT = 2.0
 LOGIT_BIAS = -4.0
 EPSILON = 1e-06
+LOG2E = 1.4426950408889634
 
 NX, NY, NZ, NC = 4, 4, 8, 2
 E, D, ROWS, Q = 1024, 768, 1536, 384
@@ -26,6 +27,9 @@
 HALF = D // 2
 BLOCK = 768
 TILE = 256
+CHUNKS = ((0, 256), (256, 512), (768, 768))
+ORDER = (0, 1, 3, 2)
+EARLY = 3
 PEERS = 1 + (NX * NY - 1) + (NZ - 1)
 
 
@@ -77,10 +81,10 @@
 
 
 def kernel(
-    queries_hbm, features_hbm, cw_hbm, tw_hbm, targets_ref, matches_ref, heads_ref, prior_ref,
+    queries_hbm, features_hbm, cw_hbm, tw_hbm, targets_hbm, matches_hbm, heads_hbm, prior_hbm,
     loss_out, query_out, class_out, box_out, side_out,
-    feat, cw, tw, own_q, all_q, unit_q, exact, inv_norm, units, hidden, raw, side,
-    cosine, grads, d_rows, d_emb, small, small_p, small_two, small_z, small_v, small_xy, small_sum,
+    targets_ref, matches_ref, heads_ref, prior_ref, feat, cw, tw, own_q, all_q, unit_q, exact, inv_norm, units, hidden, raw, side,
+    cosine, grads, sum_shift, sum_scale, d_rows, d_emb, small, small_p, small_two, small_z, small_v, small_xy, small_sum,
     small_all, q_send, q_recv, g_both, g_recv, s0, s1, r1y, r1x, t0, t1, r2a, r2b, u0, u1, r3a, r3b,
     load_sem, q_ssem, q_rsem, sp_sem, sz_ssem, sz_rsem, sxy_ssem, sxy_rsem,
     sa_ssem, sa_rsem, qs_ssem, qs_rsem, gp_ssem, gp_rsem, y1_ssem, y1_rsem, x1_ssem, x1_rsem,
@@ -110,43 +114,60 @@
         )
 
     loads = [
-        pltpu.make_async_copy(queries_hbm, own_q, load_sem.at[0]),
-        pltpu.make_async_copy(features_hbm.at[0], feat, load_sem.at[1]),
-        pltpu.make_async_copy(cw_hbm, cw, load_sem.at[2]),
-        pltpu.make_async_copy(tw_hbm, tw, load_sem.at[3]),
+        pltpu.make_async_copy(source, target, load_sem.at[i])
+        for i, (source, target) in enumerate(
+            [(cw_hbm, cw)]
+            + [
+                (features_hbm.at[0, pl.ds(start, size)], feat.at[pl.ds(start, size)])
+                for start, size in CHUNKS
+            ]
+            + [
+                (queries_hbm, own_q),
+                (heads_hbm, heads_ref),
+                (tw_hbm, tw),
+                (prior_hbm, prior_ref),
+                (targets_hbm.at[0], targets_ref),
+                (matches_hbm, matches_ref),
+            ]
+        )
     ]
-    for load in loads:
+    for load in loads[:4]:
         load.start()
 
     barrier = pltpu.get_barrier_semaphore()
     peers = [pair] + [xy_peer(dy, dx) for dy, dx in plane] + [z_peer(d) for d in zs]
     for peer in peers:
         pl.semaphore_signal(barrier, inc=1, device_id=peer, device_id_type=MESH)
-    loads[0].wait()
-    all_q[x] = own_q[...]
-    loads[1].wait()
-    loads[2].wait()
-
-    def embed(i, carry):
-        rows = rows_of(i, BLOCK)
+    def embed(start, size):
+        rows = pl.ds(start, size)
         emb = contract(feat[rows, :], cw[...], 1, 0)
         inv = lax.rsqrt(jnp.sum(emb * emb, axis=1, keepdims=True) + EPSILON)
         unit = emb * inv
         exact[rows, :] = unit
         units[rows, :] = unit.astype(BF16)
         inv_norm[rows, :] = inv
-        return carry
-
-    embed(0, 0)
-
+
+    loads[0].wait()
+    loads[1].wait()
+    for load in loads[4:]:
+        load.start()
+    embed(*CHUNKS[0])
+    loads[2].wait()
+    embed(*CHUNKS[1])
+
+    loads[4].wait()
+    all_q[0] = own_q[...]
     pl.semaphore_wait(barrier, PEERS)
-    q_copies = [
-        remote(own_q, all_q.at[x], q_ssem.at[d - 1], q_rsem.at[d - 1], x_peer(d)) for d in (1, 3, 2)
-    ]
-    for copy in q_copies:
+    q_copies = {
+        d: remote(own_q, all_q.at[ORDER.index(NX - d)], q_ssem.at[d - 1], q_rsem.at[d - 1], x_peer(d))
+        for d in (1, 3, 2)
+    }
+    for copy in q_copies.values():
         copy.start()
-    embed(1, 0)
     loads[3].wait()
+    embed(*CHUNKS[2])
+    for load in loads[5:]:
+        load.wait()
 
     def box_hidden(i, carry):
         rows = rows_of(i, BLOCK)
@@ -161,24 +182,23 @@
 
     matches = matches_ref[...]
     weight = (matches >= 0).astype(F32)
-    corners = targets_ref[0].astype(F32) * (1.0 / QUANT)
+    corners = targets_ref[...].astype(F32) * (1.0 / QUANT)
     terms, pullback = jax.vjp(
         lambda value: box_loss(value, corners, weight), raw[0:4, :] + prior_ref[...]
     )
     d_raw = (GIOU_WEIGHT * pullback(jnp.ones_like(terms))[0]).astype(BF16)
     small[0:4, :] = contract(d_raw, hidden[...], 1, 0)
 
-    for copy in q_copies:
-        copy.wait()
-    for g in range(NX):
-        rows = all_q[g].astype(F32)
+    def normalise(slot):
+        rows = all_q[slot].astype(F32)
         inv = lax.rsqrt(jnp.sum(rows * rows, axis=1, keepdims=True) + EPSILON)
-        unit_q[g * QROWS : (g + 1) * QROWS, :] = (rows * inv).astype(BF16)
+        unit_q[slot * QROWS : (slot + 1) * QROWS, :] = (rows * inv).astype(BF16)
 
     step = 32
 
-    def focal(i, loss_sum):
-        cosine[...] = contract(unit_q[...], units[rows_of(i, BLOCK), :], 1, 1)
+    def focal(first, last, i, loss_sum):
+        rows = slice(first * QROWS, last * QROWS)
+        cosine[rows, :] = contract(unit_q[rows, :], units[rows_of(i, BLOCK), :], 1, 1)
 
         def tile(n, loss_sum):
             cols = rows_of(i * (BLOCK // TILE) + n, TILE)
@@ -187,45 +207,59 @@
             pre = side[5:6, cols]
             decay = jnp.exp(jnp.minimum(pre, 0.0))
             scale = jnp.where(pre > 0, pre + 1.0, decay)
+            scale_two = scale * LOG2E
             match = matches_ref[:, cols]
 
-            def block(j, carry):
+            def block(j, target, carry):
                 loss, d_shift, d_scale = carry
                 rows = rows_of(j, step)
                 base = cosine[rows, here] + shift
-                index = lax.broadcasted_iota(jnp.int32, (step, TILE), 0)
-                hit = index == match - j * step
-                logit = base * scale
+                hit = lax.broadcasted_iota(jnp.int32, (step, TILE), 0) == target
+                logit = base * scale_two
                 value = jnp.where(hit, -logit, logit)
                 factor = jnp.where(hit, -ALPHA, 1.0 - ALPHA)
-                small_exp = jnp.exp(-jnp.abs(value))
-                log_one = jnp.log1p(small_exp)
-                big = jnp.exp(-log_one)
-                little = small_exp * big
-                positive = value >= 0
-                prob = jnp.where(positive, big, little)
-                other = jnp.where(positive, little, big)
-                neg_log = jnp.maximum(value, 0.0) + log_one
+                power = jnp.exp2(jnp.minimum(value, 100.0))
+                log_one = jnp.where(
+                    power < 2.0**-8, power * (LOG2E - power * (LOG2E / 2 - power * (LOG2E / 3))), jnp.log2(1.0 + power)
+                )
+                neg_log = jnp.maximum(log_one, value)
+                prob = jnp.exp2(value - neg_log)
+                other = jnp.exp2(-neg_log)
                 square = factor * (prob * prob)
                 loss = loss + (jnp.abs(square) * neg_log).reshape(step // 8, 8, TILE).sum(0)
-                other_log = other * neg_log
-                d_logit = square * (prob + (other_log + other_log))
+                d_logit = square * (prob + (2.0 / LOG2E) * (other * neg_log))
                 d_shift = d_shift + d_logit.reshape(step // 8, 8, TILE).sum(0)
                 d_scale = d_scale + (d_logit * base).reshape(step // 8, 8, TILE).sum(0)
                 grads[rows, cols] = (d_logit * scale).astype(BF16)
                 return loss, d_shift, d_scale
 
-            zero = jnp.zeros((8, TILE), F32)
-            loss, d_shift, d_scale = lax.fori_loop(0, Q // step, block, (loss_sum, zero, zero))
-            d_rows[0:1, cols] = jnp.sum(d_shift, axis=0, keepdims=True)
-            d_rows[1:2, cols] = jnp.sum(d_scale, axis=0, keepdims=True) * jnp.where(
-                pre > 0, 1.0, decay
+            def query_block(slot, carry):
+                owner = (x + slot + slot // 2 - 2 * (slot // 3)) % NX
+                target = match - owner * QROWS
+                for part in range(QROWS // step):
+                    carry = block(slot * (QROWS // step) + part, target - part * step, carry)
+                return carry
+
+            if first:
+                d_shift, d_scale = sum_shift[:, cols], sum_scale[:, cols]
+            else:
+                d_shift = d_scale = jnp.zeros((8, TILE), F32)
+            loss, d_shift, d_scale = lax.fori_loop(
+                first, last, query_block, (loss_sum, d_shift, d_scale)
             )
+            sum_shift[:, cols], sum_scale[:, cols] = d_shift, d_scale
             return loss
 
         return lax.fori_loop(0, BLOCK // TILE, tile, loss_sum)
 
-    focal_sum = lax.fori_loop(0, ROWS // BLOCK, focal, jnp.zeros((8, TILE), F32))
+    q_copies[1].wait_recv()
+    q_copies[3].wait_recv()
+    q_copies[2].wait_recv()
+    for slot in range(4):
+        normalise(slot)
+    focal_sum = lax.fori_loop(
+        0, ROWS // BLOCK, functools.partial(focal, 0, NX), jnp.zeros((8, TILE), F32)
+    )
 
     def embedding_grad(i, carry):
         rows = rows_of(i, BLOCK)
@@ -302,15 +336,20 @@
             q_send[g, :, cols] = part[g * QROWS : (g + 1) * QROWS, :]
     consume(3)
     qs_copies = [
-        remote(q_send.at[(x + d) % NX], q_recv.at[d - 1], qs_ssem.at[d - 1], qs_rsem.at[d - 1], x_peer(d))
+        remote(q_send.at[ORDER.index(d)], q_recv.at[d - 1], qs_ssem.at[d - 1], qs_rsem.at[d - 1], x_peer(d))
         for d in xs
     ]
     for copy in qs_copies:
         copy.start()
 
+    pre = side[5:6, :]
+    d_rows[0:1, :] = jnp.sum(sum_shift[...], axis=0, keepdims=True)
+    d_rows[1:2, :] = jnp.sum(sum_scale[...], axis=0, keepdims=True) * jnp.where(
+        pre > 0, 1.0, jnp.exp(jnp.minimum(pre, 0.0))
+    )
     small[4:6, :] = contract(d_rows[...].astype(BF16), feat[...], 1, 0)
     fold = lambda row: row[:, 0:512] + row[:, 512:1024] + row[:, 1024:1536]
-    focal_row = jnp.sum(focal_sum, axis=0, keepdims=True)
+    focal_row = jnp.sum(focal_sum, axis=0, keepdims=True) * (1.0 / LOG2E)
     small[6:7, 0:512] = GIOU_WEIGHT * fold(terms)
     small[6:7, 0:TILE] += focal_row
     small[6:7, 512:1024] = fold(weight)
@@ -384,7 +423,7 @@
 
     for copy in qs_copies:
         copy.wait_recv()
-    sums = q_send[x].astype(F32)
+    sums = q_send[0].astype(F32)
     for d in xs:
         sums = sums + q_recv[d - 1].astype(F32)
     mine = own_q[...].astype(F32)
@@ -425,7 +464,7 @@
             for h in range(2):
                 distance, move = z_copy(half, k, h)
                 pl.when(distance != 0)(move.wait_send)
-    for copy in qs_copies + sz_copies + sxy_copies + sa_copies + f0_copies:
+    for copy in list(q_copies.values()) + qs_copies + sz_copies + sxy_copies + sa_copies + f0_copies:
         copy.wait_send()
     for target in range(NX):
         itself = jnp.logical_and(y == x, x == target)
@@ -452,9 +491,13 @@
             jax.ShapeDtypeStruct((4, E), F32),
             jax.ShapeDtypeStruct((2, E), F32),
         ),
-        in_specs=[hbm] * 4 + [vmem] * 4,
+        in_specs=[hbm] * 8,
         out_specs=[vmem] * 5,
         scratch_shapes=[
+            buf(jnp.int32, 4, ROWS),
+            buf(jnp.int32, 1, ROWS),
+            buf(BF16, 6, E),
+            buf(F32, 4, ROWS),
             buf(BF16, ROWS, E),
             buf(BF16, E, D),
             buf(BF16, E, E),
@@ -469,6 +512,8 @@
             buf(F32, 6, ROWS),
             buf(F32, Q, BLOCK),
             buf(BF16, Q, ROWS),
+            buf(F32, 8, ROWS),
+            buf(F32, 8, ROWS),
             buf(F32, 2, ROWS),
             buf(BF16, ROWS, D),
             buf(F32, 8, E),
@@ -495,7 +540,7 @@
             buf(BF16, SHARE, HALF),
             buf(BF16, NX - 1, SHARE, HALF),
             buf(BF16, NY, SHARE, HALF),
-            dma(4), dma(NX - 1), dma(NX - 1), dma(2),
+            dma(10), dma(NX - 1), dma(NX - 1), dma(2),
             dma(NZ - 1), dma(NZ - 1), dma(NY, NX), dma(NY, NX),
             dma(NZ - 1), dma(NZ - 1), dma(NX - 1), dma(NX - 1), dma(NX), dma(NX),
             dma(NY - 1, NX), dma(NY - 1, NX), dma(NX - 1, NX), dma(NX - 1, NX),

time: 57 us -> 54.5 us (0.956)
  Pallas kernels: 56.2 us -> 53.7 us
    pallas_call x1, Pallas kernels: 53.8 us -> 51.4 us  [on_device(): pl.pallas_call(kernel, out_shape=(jax.ShapeDtypeStruct((1, 1), F32), jax....]
where the time goes in v3:
time: 54.5 us; the launch traced here: 54.4 us
  Pallas kernels  53.7 us (99%)
  between operations  0.64 us (1%)
    pallas_call x1, Pallas kernels, on_device(): pl.pallas_call(kernel, out_shape=(jax.ShapeDtypeStruct((1, 1), F32), jax....  51.4 us
    pallas_call x1, Pallas kernels, on_device(): pl.pallas_call(finish, out_shape=tuple((jax.ShapeDtypeStruct(r.shape, F32...  2.37 us

profile of v3, /device:TPU:2, one launch (start us, length us, event | category | flops | bytes accessed | tf_op | source)
XLA Modules:
  0.0 54.4 jit_solution(6998276529558731466)
XLA Ops:
  0.6 51.4 %shard_map.119 = (f32[1,1]{1,0:T(1,128)}, f32[96,768]{1,0:T(8,128)}, f32[16,768]{1,0:T(8,128)}, f32[4,1024]{1,0:T(4,128)}, f32[2,1024]{1,0:T(2,128)}) custom-call(bf16[96,768]{1,0:T(8,128)(2,1)} %queries_hbm.1, bf16[1,1536,1024]{2,1,0:T(8,128)(2,1)} %features_hbm.1, bf16[1024,768]{1,0:T(8,128)(2,1)} %cw_hbm.1, bf16[1024,1024]{1,0:T(8,128)(2,1)} %tw_hbm.1, ...), custom_call_target="tpu_custom_call" | custom-call | flops 11000000512 | bytes 8000000 | tf_op jit(solution)/shard_map/pallas_call | solution.py:485
  52.0 2.4 %shard_map.120 = (f32[1,1]{1,0:T(1,128)}, f32[96,768]{1,0:T(8,128)}, f32[16,768]{1,0:T(8,128)}, f32[4,1024]{1,0:T(4,128)}, f32[2,1024]{1,0:T(2,128)}) custom-call(f32[1,1]{1,0:T(1,128)} %get-tuple-element.15.refs_0_, f32[96,768]{1,0:T(8,128)} %get-tuple-element.16.refs_1_, f32[16,768]{1,0:T(8,128)} %get-tuple-element.17.refs_2_, ...), custom_call_target="tpu_custom_call" | custom-call | tf_op jit(solution)/shard_map/pallas_call | solution.py:561

commit v4 on v3

--- a/solution.py
+++ b/solution.py
@@ -329,19 +329,6 @@
     produce(3)
     consume(2)
 
-    for n in range(D // TILE):
-        cols = slice(n * TILE, (n + 1) * TILE)
-        part = contract(grads[...], units[:, cols], 1, 0).astype(BF16)
-        for g in range(NX):
-            q_send[g, :, cols] = part[g * QROWS : (g + 1) * QROWS, :]
-    consume(3)
-    qs_copies = [
-        remote(q_send.at[ORDER.index(d)], q_recv.at[d - 1], qs_ssem.at[d - 1], qs_rsem.at[d - 1], x_peer(d))
-        for d in xs
-    ]
-    for copy in qs_copies:
-        copy.start()
-
     pre = side[5:6, :]
     d_rows[0:1, :] = jnp.sum(sum_shift[...], axis=0, keepdims=True)
     d_rows[1:2, :] = jnp.sum(sum_scale[...], axis=0, keepdims=True) * jnp.where(
@@ -357,7 +344,7 @@
     small_pair = remote(small, small_p, sp_sem.at[0], sp_sem.at[1], pair)
     small_pair.start()
 
-    forward(0)
+    consume(3)
     small_pair.wait()
     for k in range(NZ):
         lanes = slice(k * 128, (k + 1) * 128)
@@ -368,9 +355,20 @@
     ]
     for copy in sz_copies:
         copy.start()
-    for k in range(1, NX):
+    for n in range(D // TILE):
+        cols = slice(n * TILE, (n + 1) * TILE)
+        part = contract(grads[...], units[:, cols], 1, 0).astype(BF16)
+        for g in range(NX):
+            q_send[g, :, cols] = part[g * QROWS : (g + 1) * QROWS, :]
+    qs_copies = [
+        remote(q_send.at[ORDER.index(d)], q_recv.at[d - 1], qs_ssem.at[d - 1], qs_rsem.at[d - 1], x_peer(d))
+        for d in xs
+    ]
+    for copy in qs_copies:
+        copy.start()
+
+    for k in range(NX):
         forward(k)
-
     for copy in sz_copies:
         copy.wait_recv()
     small_v[...] = (
@@ -485,11 +483,11 @@
     loss, query, classes, box, side = pl.pallas_call(
         kernel,
         out_shape=(
-            jax.ShapeDtypeStruct((1, 1), F32),
-            jax.ShapeDtypeStruct((QROWS, D), F32),
-            jax.ShapeDtypeStruct((SHARE, D), F32),
-            jax.ShapeDtypeStruct((4, E), F32),
-            jax.ShapeDtypeStruct((2, E), F32),
+            pltpu.VMEM((1, 1), F32),
+            pltpu.VMEM((QROWS, D), F32),
+            pltpu.VMEM((SHARE, D), F32),
+            pltpu.VMEM((4, E), F32),
+            pltpu.VMEM((2, E), F32),
         ),
         in_specs=[hbm] * 8,
         out_specs=[vmem] * 5,
@@ -557,7 +555,9 @@
         queries, features, class_weight, trunk_weight, targets, matches, head_rows,
         jnp.asarray(box_prior(ROWS)),
     )
-    results = (loss, query, classes, box, side)
+    results = tuple(
+        pltpu.with_memory_space_constraint(r, pltpu.VMEM) for r in (loss, query, classes, box, side)
+    )
     loss, query, classes, box, side = pl.pallas_call(
         finish,
         out_shape=tuple(jax.ShapeDtypeStruct(r.shape, F32) for r in results),

time: 54.5 us -> 53.3 us (0.978)
  Pallas kernels: 53.7 us -> 52.3 us
    pallas_call x1, Pallas kernels: 2.37 us -> 1.38 us  [on_device(): pl.pallas_call(finish, out_shape=tuple((jax.ShapeDtypeStruct(r.shape, F32...]
where the time goes in v4:
time: 53.3 us; the launch traced here: 53 us
  Pallas kernels  52.3 us (98%)
  between operations  0.64 us (1%)
    pallas_call x1, Pallas kernels, on_device(): pl.pallas_call(kernel, out_shape=(pltpu.VMEM((1, 1), F32), pltpu.VMEM((QR...  51 us
    pallas_call x1, Pallas kernels, on_device(): pl.pallas_call(finish, out_shape=tuple((jax.ShapeDtypeStruct(r.shape, F32...  1.38 us

profile of v4, /device:TPU:2, one launch (start us, length us, event | category | flops | bytes accessed | tf_op | source)
XLA Modules:
  0.0 53.0 jit_solution(12044537146099516761)
XLA Ops:
  0.6 51.0 %shard_map.119 = (f32[1,1]{1,0:T(1,128)}, f32[96,768]{1,0:T(8,128)S(1)}, f32[16,768]{1,0:T(8,128)S(1)}, f32[4,1024]{1,0:T(4,128)S(1)}, f32[2,1024]{1,0:T(2,128)S(1)}) custom-call(bf16[96,768]{1,0:T(8,128)(2,1)} %queries_hbm.1, bf16[1,1536,1024]{2,1,0:T(8,128)(2,1)} %features_hbm.1, bf16[1024,768]{1,0:T(8,128)(2,1)} %cw_hbm.1, bf16[1024,1024]{1,0:T(8,128)(2,1)} %tw_hbm.1, ...), custom_call_target="tpu_custom_call" | custom-call | flops 11000000512 | bytes 8000000 | tf_op jit(solution)/shard_map/pallas_call | solution.py:483
  51.6 1.4 %shard_map.120 = (f32[1,1]{1,0:T(1,128)}, f32[96,768]{1,0:T(8,128)}, f32[16,768]{1,0:T(8,128)}, f32[4,1024]{1,0:T(4,128)}, f32[2,1024]{1,0:T(2,128)}) custom-call(f32[1,1]{1,0:T(1,128)} %get-tuple-element.15.refs_0_, f32[96,768]{1,0:T(8,128)S(1)} %get-tuple-element.16.refs_1_, f32[16,768]{1,0:T(8,128)S(1)} %get-tuple-element.17.refs_2_, ...), custom_call_target="tpu_custom_call" | custom-call | tf_op jit(solution)/shard_map/pallas_call | solution.py:561

commit v5 on v4

--- a/solution.py
+++ b/solution.py
@@ -292,9 +292,12 @@
         left = jnp.concatenate(
             [feat[:, k * 128 : (k + 1) * 128], feat[:, (k + NX) * 128 : (k + NX + 1) * 128]], axis=1
         )
-        part = contract(left, d_emb[...], 0, 0).astype(BF16).reshape(2, NY, NC, SHARE, D)
-        for cc in range(NC):
-            g_both[cc, k] = part[:, :, cc]
+        for n in range(D // TILE):
+            cols = slice(n * TILE, (n + 1) * TILE)
+            part = contract(left, d_emb[:, cols], 0, 0).astype(BF16)
+            part = part.reshape(2, NY, NC, SHARE, TILE)
+            for cc in range(NC):
+                g_both[cc, k, :, :, :, cols] = part[:, :, cc]
         pair_copy(k).start()
 
     def consume(k):

time: 53.3 us -> 53.3 us (level)
  no operation moved by 1% of the time
where the time goes in v5:
time: 53.3 us; the launch traced here: 53 us
  Pallas kernels  52.3 us (98%)
  between operations  0.64 us (1%)
    pallas_call x1, Pallas kernels, on_device(): pl.pallas_call(kernel, out_shape=(pltpu.VMEM((1, 1), F32), pltpu.VMEM((QR...  51 us
    pallas_call x1, Pallas kernels, on_device(): pl.pallas_call(finish, out_shape=tuple((jax.ShapeDtypeStruct(r.shape, F32...  1.38 us

profile of v5, /device:TPU:2, one launch (start us, length us, event | category | flops | bytes accessed | tf_op | source)
XLA Modules:
  0.0 53.0 jit_solution(12044537146099516761)
XLA Ops:
  0.6 51.0 %shard_map.119 = (f32[1,1]{1,0:T(1,128)}, f32[96,768]{1,0:T(8,128)S(1)}, f32[16,768]{1,0:T(8,128)S(1)}, f32[4,1024]{1,0:T(4,128)S(1)}, f32[2,1024]{1,0:T(2,128)S(1)}) custom-call(bf16[96,768]{1,0:T(8,128)(2,1)} %queries_hbm.1, bf16[1,1536,1024]{2,1,0:T(8,128)(2,1)} %features_hbm.1, bf16[1024,768]{1,0:T(8,128)(2,1)} %cw_hbm.1, bf16[1024,1024]{1,0:T(8,128)(2,1)} %tw_hbm.1, ...), custom_call_target="tpu_custom_call" | custom-call | flops 11000000512 | bytes 8000000 | tf_op jit(solution)/shard_map/pallas_call | solution.py:486
  51.6 1.4 %shard_map.120 = (f32[1,1]{1,0:T(1,128)}, f32[96,768]{1,0:T(8,128)}, f32[16,768]{1,0:T(8,128)}, f32[4,1024]{1,0:T(4,128)}, f32[2,1024]{1,0:T(2,128)}) custom-call(f32[1,1]{1,0:T(1,128)} %get-tuple-element.15.refs_0_, f32[96,768]{1,0:T(8,128)S(1)} %get-tuple-element.16.refs_1_, f32[16,768]{1,0:T(8,128)S(1)} %get-tuple-element.17.refs_2_, ...), custom_call_target="tpu_custom_call" | custom-call | tf_op jit(solution)/shard_map/pallas_call | solution.py:564
